TPU v7x, 128 devices: a whole 4x4x4 slice. The times are simulated.
128 devices in a mesh: dp: 4 (over x), seq: 32 (over z, y, core).
Axes of the slice: x: 4, y: 4, z: 4, core: 2. Of those that a mesh axis runs over, the one named last changes fastest.
Arguments:
- tile_feats: bfloat16 [65536, 1536], P(('dp', 'seq')), may hold values from -6 to 6, as said below
- tile_dest: int32 [65536, 1], P(('dp', 'seq')), may hold values from 0 to 127; in each aligned block of 512 rows (0 to 511, 512 to 1023, ...) at most 8 rows name the same one
- embed_weight: bfloat16 [1536, 768], replicated, may hold values from -0.15625 to 0.15625
- norm1_gain: float32 [768], replicated, may hold values from 0.1 to 1.9
- qkv_weight: bfloat16 [768, 2304], replicated, may hold values from -0.21875 to 0.21875
- out_weight: bfloat16 [768, 768], replicated, may hold values from -0.21875 to 0.21875
- norm2_gain: float32 [768], replicated, may hold values from 0.1 to 1.9
- up_weight: bfloat16 [768, 3072], replicated, may hold values from -0.21875 to 0.21875
- down_weight: bfloat16 [3072, 768], replicated, may hold values from -0.109375 to 0.109375
Outputs:
- tile_out: bfloat16 [65536, 768], P(('dp', 'seq'))
- far_heads: float32 [4, 16, 512, 48], P('dp', None, 'seq')
Inputs may be any that keep to these rules, and one draw needn't show every extreme that they name: `tile_dest`: destination devices are numbered over dp then seq. Among the 512 tiles of one device at most 8 name the same destination, and some device reaches 8; every device is named by some tile. `tile_feats`: some tiles' embeddings are entirely zero; they are real tiles like any other.
All inputs are finite; a program needn't handle non-finite values.
Results may differ from a plain program's by a relative error of at most 0.012.
Values may be sent and summed in bfloat16 or wider, within the bound.
A program may use at most 128 MiB of HBM per device.

v0:
```python
import functools
import math

import jax
import jax.numpy as jnp
from jax import lax
from jax.experimental import pallas as pl
from jax.experimental.pallas import tpu as pltpu
from jax.sharding import PartitionSpec as P

F32 = jnp.float32
BF16 = jnp.bfloat16
MESH = pl.DeviceIdType.MESH
HEADS = 16
HEAD = 48
D = 768
F = 1536
FF = 3072
TILES = 512
SLOTS = 1024
CAP = 8
N_DP = 4
N_SEQ = 32
DEVICES = 128
RATE = 64
ROWS = SLOTS // RATE
QUERIES = 512
FF_BLOCK = 512
EPSILON = 1e-5
MASKED = -1e30
EMPTY = 1e30
SCALE = HEAD ** -0.5 * math.log2(math.e)
NT = (((1,), (1,)), ((), ()))
TN = (((0,), (0,)), ((), ()))


def dot(a, b):
    return jnp.dot(a, b, preferred_element_type=F32)


def iota(shape, axis):
    return lax.broadcasted_iota(jnp.int32, shape, axis)


def layer_norm(x, gain):
    centred = x - jnp.mean(x, axis=1, keepdims=True)
    spread = jnp.mean(centred * centred, axis=1, keepdims=True)
    return (centred * lax.rsqrt(spread + EPSILON) * gain).astype(BF16)


def to_message(rows):
    n, w = rows.shape
    left = rows[:, : w // 2].reshape(n // CAP, CAP, w // 2)
    right = rows[:, w // 2 :].reshape(n // CAP, CAP, w // 2)
    return jnp.concatenate([left, right], axis=1).astype(BF16)


def from_message(message):
    n, _, w = message.shape
    wide = message.astype(F32)
    left = wide[:, :CAP].reshape(n * CAP, w)
    right = wide[:, CAP:].reshape(n * CAP, w)
    return jnp.concatenate([left, right], axis=1)


def kernel(
    feats_hbm, dest_ref, embed_hbm, gain1_ref, qkv_hbm, out_hbm, gain2_ref, up_hbm, down_hbm,
    tile_ref, far_ref,
    feats, embed_w, qkv_w, out_w, up_w, down_w, qkv_t,
    embedded, normed, slot_col, send1, recv1, x_ref, bias_ref,
    q_t, k_ref, v_t, scores, near, peak, mixed,
    far_send, far_recv, res_send, res_recv, far_t,
    send2, recv2, hidden, total,
    load_sem, send1_sem, recv1_sem, fsend_sem, frecv_sem, rsend_sem, rrecv_sem, send2_sem, recv2_sem,
):
    dp, sq = lax.axis_index("dp"), lax.axis_index("seq")
    me = dp * N_SEQ + sq

    def partner(k):
        k = (k * 37) % DEVICES
        x = (dp + k // 32) % 4
        z = (sq // 8 + (k // 8) % 4) % 4
        y = (sq // 2 + (k // 2) % 4) % 4
        return x, z * 8 + y * 2 + (sq + k) % 2

    loads = [
        pltpu.make_async_copy(src, dst, load_sem.at[i])
        for i, (src, dst) in enumerate(
            [(feats_hbm, feats), (embed_hbm, embed_w), (qkv_hbm, qkv_w), (out_hbm, out_w), (up_hbm, up_w), (down_hbm, down_w)]
        )
    ]
    for load in loads:
        load.start()

    barrier = pltpu.get_barrier_semaphore()

    def greet(k, carry):
        x, s = partner(k)
        pl.semaphore_signal(barrier, inc=1, device_id=(x, s), device_id_type=MESH)
        return carry

    lax.fori_loop(1, DEVICES, greet, 0)

    dest = dest_ref[...]
    onehot = (dest == iota((TILES, DEVICES), 1)).astype(F32)
    below = (iota((TILES, TILES), 1) < iota((TILES, TILES), 0)).astype(BF16)
    rank = jnp.sum(dot(below, onehot.astype(BF16)) * onehot, axis=1, keepdims=True)
    slots = dest.astype(F32) * CAP + rank
    slot_col[...] = jnp.broadcast_to(slots, (TILES, 128))
    slot_row = jnp.transpose(slot_col[...])[0:1, :].astype(jnp.int32)

    loads[0].wait()
    loads[1].wait()
    for i in range(4):
        rows = pl.ds(i * 128, 128)
        tile_rows = dot(feats[rows, :], embed_w[...]).astype(BF16)
        embedded[rows, :] = tile_rows
        normed[rows, :] = layer_norm(tile_rows.astype(F32), gain1_ref[...])

    def pack(i, carry):
        place = (iota((256, TILES), 0) + i * 256 == slot_row).astype(F32)
        rows = dot(place.astype(BF16), normed[...])
        used = jnp.sum(place, axis=1, keepdims=True)
        first = jnp.where((iota((256, 128), 1) == 0) & (used < 0.5), EMPTY, rows[:, :128])
        send1[pl.ds(i * 32, 32)] = to_message(jnp.concatenate([first, rows[:, 128:]], axis=1))
        return carry

    lax.fori_loop(0, 4, pack, 0)
    pl.semaphore_wait(barrier, DEVICES - 1)

    def send_rows(k, carry):
        x, s = partner(k)
        pltpu.make_async_remote_copy(
            src_ref=send1.at[x * N_SEQ + s], dst_ref=recv1.at[me], send_sem=send1_sem, recv_sem=recv1_sem.at[me],
            device_id=(x, s), device_id_type=MESH,
        ).start()
        return carry

    lax.fori_loop(1, DEVICES, send_rows, 0)
    pltpu.make_async_copy(send1.at[me], recv1.at[me], recv1_sem.at[me]).start()

    loads[2].wait()

    def turn(i, carry):
        columns = pl.ds(pl.multiple_of(i * 128, 128), 128)
        qkv_t[columns, :] = jnp.transpose(qkv_w[:, columns].astype(F32)).astype(BF16)
        return carry

    lax.fori_loop(0, 3 * D // 128, turn, 0)
    one_row = (iota((16, SLOTS), 0) == 0).astype(BF16)
    for h in range(HEADS):
        base = 64 * (h % 2)
        q_t[h, pl.ds(64 - base, 64), :] = jnp.zeros((64, SLOTS), BF16)
        q_t[h, pl.ds(base + HEAD, 16), :] = one_row
        v_t[h, pl.ds(HEAD, 16), :] = jnp.ones((16, SLOTS), BF16)

    def arrived1(s, carry):
        pltpu.make_async_copy(send1.at[s], recv1.at[s], recv1_sem.at[s]).wait()
        return carry

    lax.fori_loop(0, DEVICES, arrived1, 0)

    def project(g, carry):
        rows = from_message(recv1[pl.ds(g * 32, 32)])
        empty = rows[:, 0:1] > 0.1 * EMPTY
        rows = jnp.where(empty, 0.0, rows).astype(BF16)
        bias = jnp.broadcast_to(jnp.where(empty, MASKED, 0.0), (256, 128))
        x_ref[pl.ds(g * 4, 4)] = rows.reshape(4, RATE, D)
        bias_ref[pl.ds(g * 4, 4)] = bias.astype(BF16).reshape(4, RATE, 128)
        lanes = pl.ds(pl.multiple_of(g * 256, 256), 256)
        query = (lax.dot_general(qkv_t[0:D, :], rows, NT, preferred_element_type=F32) * SCALE).astype(BF16)
        for h in range(HEADS):
            q_t[h, pl.ds(64 * (h % 2), HEAD), lanes] = query[h * HEAD : (h + 1) * HEAD]
        key = lax.dot_general(qkv_t[D : 2 * D, :], rows, NT, preferred_element_type=F32)
        masks = jnp.where(iota((16, 256), 0) == 0, jnp.transpose(bias)[0:16, :], 0.0)
        for p in range(HEADS // 2):
            pair = jnp.concatenate(
                [key[96 * p : 96 * p + 48], masks, key[96 * p + 48 : 96 * p + 96], masks], axis=0
            )
            k_ref[p, pl.ds(pl.multiple_of(g * 256, 256), 256), :] = jnp.transpose(pair).astype(BF16)
        value = lax.dot_general(qkv_t[2 * D :, :], rows, NT, preferred_element_type=F32).astype(BF16)
        for h in range(HEADS):
            v_t[h, pl.ds(0, HEAD), lanes] = value[h * HEAD : (h + 1) * HEAD]
        return carry

    lax.fori_loop(0, 4, project, 0)

    rows = x_ref[:, pl.ds(0, 16), :].reshape(256, D)
    swap = (iota((256, 256), 1) == (iota((256, 256), 0) & 15) * 16 + (iota((256, 256), 0) >> 4)).astype(BF16)
    rows = dot(swap, rows).astype(BF16)
    bias = dot(swap, bias_ref[:, pl.ds(0, 16), :].reshape(256, 128))
    low = HEAD * (iota((256, D), 0) >> 4)
    column = iota((256, D), 1)
    own = (column >= low) & (column < low + HEAD)
    turns = (iota((D, 128), 0) - iota((D, 128), 1)).astype(F32) * (1.0 / HEAD)
    whole = jnp.abs(turns - jnp.round(turns)) < 0.01
    lane = iota((D, 128), 1)
    to_front = (whole & (lane < HEAD)).astype(BF16)
    turns = turns + (64.0 / HEAD)
    whole = jnp.abs(turns - jnp.round(turns)) < 0.01
    to_back = (whole & (lane >= 64) & (lane < 64 + HEAD)).astype(BF16)

    def own_head(part, scale):
        product = dot(rows, qkv_w[:, part * D : (part + 1) * D]) * scale
        return jnp.where(own, product, 0.0).astype(BF16)

    lane = iota((256, 128), 1)
    far_q = jnp.where(lane == HEAD, 1.0, dot(own_head(0, SCALE), to_front))
    far_kv = dot(own_head(1, 1.0), to_front) + dot(own_head(2, 1.0), to_back)
    far_kv = jnp.where(lane == HEAD, bias, jnp.where(lane == 64 + HEAD, 1.0, far_kv))
    far_send[...] = jnp.concatenate(
        [far_q.reshape(HEADS, ROWS, 128), far_kv.reshape(HEADS, ROWS, 128)], axis=1
    ).astype(BF16)

    def send_far(h, carry):
        @pl.when(2 * h != sq)
        def _():
            pltpu.make_async_remote_copy(
                src_ref=far_send.at[h], dst_ref=far_recv.at[sq], send_sem=fsend_sem, recv_sem=frecv_sem.at[sq],
                device_id=(dp, 2 * h), device_id_type=MESH,
            ).start()

        @pl.when(2 * h == sq)
        def _():
            pltpu.make_async_copy(far_send.at[h], far_recv.at[sq], frecv_sem.at[sq]).start()

        return carry

    lax.fori_loop(0, HEADS, send_far, 0)

    parts = SLOTS // QUERIES

    def score(h, i):
        return lax.dot_general(
            k_ref[h // 2], q_t[h, :, i * QUERIES : (i + 1) * QUERIES], (((1,), (0,)), ((), ())), preferred_element_type=F32
        )

    def attend(first, last):
        scores[0] = score(first, 0)

        def one_head(h, carry):
            for i in range(parts):
                if i + 1 < parts:
                    later = score(h, i + 1)
                else:
                    later = score(jnp.minimum(h + 1, last - 1), 0)
                block = scores[i % 2]
                top = jnp.max(block, axis=0, keepdims=True)
                weights = jnp.exp2(block - top).astype(BF16)
                near[h, :, i * QUERIES : (i + 1) * QUERIES] = dot(v_t[h], weights)
                peak[h, :, i * QUERIES : (i + 1) * QUERIES] = jnp.broadcast_to(top, (8, QUERIES))
                scores[(i + 1) % 2] = later
            return carry

        lax.fori_loop(first, last, one_head, 0)

    def far_branch():
        def arrived(s, carry):
            pltpu.make_async_copy(far_recv.at[s], far_recv.at[s], frecv_sem.at[s]).wait()
            return carry

        lax.fori_loop(0, N_SEQ, arrived, 0)
        queries = far_recv[:, pl.ds(0, 16), :].reshape(N_SEQ * ROWS, 128)
        pairs = far_recv[:, pl.ds(16, 16), :].reshape(N_SEQ * ROWS, 128)
        block = lax.dot_general(queries, pairs, NT, preferred_element_type=F32)
        top = jnp.max(block, axis=1, keepdims=True)
        result = dot(jnp.exp2(block - top).astype(BF16), pairs)
        summed = result[:, 64 + HEAD : 65 + HEAD]
        result = jnp.where(iota(result.shape, 1) < 64, top + jnp.log2(summed), result / summed)
        res_send[...] = result.reshape(N_SEQ, ROWS, 128)
        head = sq // 2

        def answer(s, carry):
            @pl.when(s != sq)
            def _():
                pltpu.make_async_remote_copy(
                    src_ref=res_send.at[s], dst_ref=res_recv.at[head], send_sem=rsend_sem, recv_sem=rrecv_sem.at[head],
                    device_id=(dp, s), device_id_type=MESH,
                ).start()

            return carry

        lax.fori_loop(0, N_SEQ, answer, 0)
        pltpu.make_async_copy(res_send.at[sq], res_recv.at[head], rrecv_sem.at[head]).start()
        pltpu.make_async_copy(
            res_send.at[pl.ds(0, N_SEQ - 1)], res_send.at[pl.ds(0, N_SEQ - 1)], rsend_sem
        ).wait()

    def far_arrived():
        def arrived(h, carry):
            pltpu.make_async_copy(res_recv.at[h], res_recv.at[h], rrecv_sem.at[h]).wait()
            return carry

        lax.fori_loop(0, HEADS, arrived, 0)
        results = res_recv[...].reshape(HEADS * ROWS, 128)
        far_ref[...] = res_recv[:, :, 64 : 64 + HEAD]
        lane = iota((HEADS * ROWS, 128), 1)
        high = results.astype(BF16).astype(F32)
        middle = (results - high).astype(BF16).astype(F32)
        lowest = results - high - middle
        split = jnp.where(lane >= 64, results, jnp.where(lane == 0, high, jnp.where(lane == 1, middle, lowest)))
        row = iota((HEADS * ROWS, SLOTS), 0)
        spread = (iota((HEADS * ROWS, SLOTS), 1) == (row & 15) * RATE + (row >> 4)).astype(BF16)
        far_t[...] = lax.dot_general(split.astype(BF16), spread, TN, preferred_element_type=F32)

    def blend(first, last):
        def one_head(h, carry):
            summed = near[h, HEAD : HEAD + 1, :]
            near_lse = peak[h, 0:1, :] + jnp.log2(summed)
            far_lse = far_t[0:1, :] + far_t[1:2, :] + far_t[2:3, :]
            far_lse = jnp.where((iota((1, SLOTS), 1) & (RATE - 1)) == h, far_lse, MASKED)
            larger = jnp.maximum(near_lse, far_lse)
            near_weight = jnp.exp2(near_lse - larger)
            far_weight = jnp.exp2(far_lse - larger)
            both = near_weight + far_weight
            joined = near[h, 0:HEAD, :] * (near_weight / (both * summed)) + far_t[64 : 64 + HEAD, :] * (far_weight / both)
            mixed[pl.ds(pl.multiple_of(h * HEAD, 16), HEAD), :] = joined.astype(BF16)
            return carry

        lax.fori_loop(first, last, one_head, 0)

    def give_back(c):
        def pack_back(g, carry):
            lanes = pl.ds(pl.multiple_of(g * 256, 256), 256)
            rows = jnp.transpose(mixed[256 * c : 256 * (c + 1), lanes].astype(F32))
            send2[c, pl.ds(g * 32, 32)] = to_message(rows)
            return carry

        lax.fori_loop(0, 4, pack_back, 0)

        def send_back(k, carry):
            x, s = partner(k)
            pltpu.make_async_remote_copy(
                src_ref=send2.at[c, x * N_SEQ + s], dst_ref=recv2.at[c, me], send_sem=send2_sem.at[c], recv_sem=recv2_sem.at[c, me],
                device_id=(x, s), device_id_type=MESH,
            ).start()
            return carry

        lax.fori_loop(1, DEVICES, send_back, 0)
        pltpu.make_async_copy(send2.at[c, me], recv2.at[c, me], recv2_sem.at[c, me]).start()

    attend(0, 3)

    @pl.when(sq % 2 == 0)
    def _():
        far_branch()

    attend(3, 6)
    far_arrived()
    blend(0, 6)
    give_back(0)
    attend(6, 11)
    blend(6, 11)
    give_back(1)
    attend(11, 16)
    blend(11, 16)
    give_back(2)

    loads[3].wait()
    hidden[...] = embedded[...].astype(F32)
    for c in range(3):
        def arrived2(s, carry, c=c):
            pltpu.make_async_copy(send2.at[c, s], recv2.at[c, s], recv2_sem.at[c, s]).wait()
            return carry

        lax.fori_loop(0, DEVICES, arrived2, 0)
        taken = jnp.zeros((TILES, 256), F32)
        for g in range(4):
            place = (iota((TILES, 256), 1) + g * 256 == slot_col[:, 0:1].astype(jnp.int32)).astype(BF16)
            taken = taken + dot(place, from_message(recv2[c, pl.ds(g * 32, 32)]).astype(BF16))
        hidden[...] += dot(taken.astype(BF16), out_w[256 * c : 256 * (c + 1), :])
    loads[4].wait()
    loads[5].wait()
    state = hidden[...].astype(BF16).astype(F32)
    normed[...] = layer_norm(state, gain2_ref[...])
    total[...] = state

    def feed(i, carry):
        columns = pl.ds(pl.multiple_of(i * FF_BLOCK, FF_BLOCK), FF_BLOCK)
        inner = dot(normed[...], up_w[:, columns])
        inner = jax.nn.gelu(inner, approximate=True).astype(BF16)
        total[...] += dot(inner, down_w[columns, :])
        return carry

    lax.fori_loop(0, FF // FF_BLOCK, feed, 0)
    tile_ref[...] = total[...].astype(BF16)

    most = pl.ds(0, DEVICES - 1)
    pltpu.make_async_copy(send1.at[most], send1.at[most], send1_sem).wait()
    for c in range(3):
        pltpu.make_async_copy(send2.at[c, most], send2.at[c, most], send2_sem.at[c]).wait()

    @pl.when(sq % 2 == 0)
    def _():
        pltpu.make_async_copy(far_send.at[pl.ds(0, 15)], far_send.at[pl.ds(0, 15)], fsend_sem).wait()

    @pl.when(sq % 2 == 1)
    def _():
        pltpu.make_async_copy(far_send, far_send, fsend_sem).wait()


def on_device(tile_feats, tile_dest, embed_weight, norm1_gain, qkv_weight, out_weight, norm2_gain, up_weight, down_weight):
    hbm = pl.BlockSpec(memory_space=pl.ANY)
    vmem = pl.BlockSpec(memory_space=pltpu.VMEM)
    dma = pltpu.SemaphoreType.DMA
    tile_out, far_heads = pl.pallas_call(
        kernel,
        out_shape=(
            jax.ShapeDtypeStruct((TILES, D), BF16),
            jax.ShapeDtypeStruct((HEADS, ROWS, HEAD), F32),
        ),
        in_specs=[hbm, vmem, hbm, vmem, hbm, hbm, vmem, hbm, hbm],
        out_specs=(vmem, vmem),
        scratch_shapes=[
            pltpu.VMEM((TILES, F), BF16),
            pltpu.VMEM((F, D), BF16),
            pltpu.VMEM((D, 3 * D), BF16),
            pltpu.VMEM((D, D), BF16),
            pltpu.VMEM((D, FF), BF16),
            pltpu.VMEM((FF, D), BF16),
            pltpu.VMEM((3 * D, D), BF16),
            pltpu.VMEM((TILES, D), BF16),
            pltpu.VMEM((TILES, D), BF16),
            pltpu.VMEM((TILES, 128), F32),
            pltpu.VMEM((DEVICES, 16, 384), BF16),
            pltpu.VMEM((DEVICES, 16, 384), BF16),
            pltpu.VMEM((ROWS, RATE, D), BF16),
            pltpu.VMEM((ROWS, RATE, 128), BF16),
            pltpu.VMEM((HEADS, 128, SLOTS), BF16),
            pltpu.VMEM((HEADS // 2, SLOTS, 128), BF16),
            pltpu.VMEM((HEADS, 64, SLOTS), BF16),
            pltpu.VMEM((2, SLOTS, QUERIES), F32),
            pltpu.VMEM((HEADS, 64, SLOTS), F32),
            pltpu.VMEM((HEADS, 8, SLOTS), F32),
            pltpu.VMEM((D, SLOTS), BF16),
            pltpu.VMEM((HEADS, 32, 128), BF16),
            pltpu.VMEM((N_SEQ, 32, 128), BF16),
            pltpu.VMEM((N_SEQ, ROWS, 128), F32),
            pltpu.VMEM((HEADS, ROWS, 128), F32),
            pltpu.VMEM((128, SLOTS), F32),
            pltpu.VMEM((3, DEVICES, 16, 128), BF16),
            pltpu.VMEM((3, DEVICES, 16, 128), BF16),
            pltpu.VMEM((TILES, D), F32),
            pltpu.VMEM((TILES, D), F32),
            dma((6,)),
            dma,
            dma((DEVICES,)),
            dma,
            dma((N_SEQ,)),
            dma,
            dma((HEADS,)),
            dma((3,)),
            dma((3, DEVICES)),
        ],
        compiler_params=pltpu.CompilerParams(collective_id=0, has_side_effects=True, vmem_limit_bytes=62 << 20),
    )(
        tile_feats, tile_dest, embed_weight, norm1_gain.reshape(1, D), qkv_weight, out_weight,
        norm2_gain.reshape(1, D), up_weight, down_weight,
    )
    return tile_out, far_heads[None]


def solution(mesh):
    return jax.shard_map(
        on_device,
        mesh=mesh,
        in_specs=(P(("dp", "seq"), None), P(("dp", "seq"), None), P(), P(), P(), P(), P(), P(), P()),
        out_specs=(P(("dp", "seq"), None), P("dp", None, "seq", None)),
        check_vma=False,
    )
```

profile of v0, /device:TPU:1, one launch (start us, length us, event | category | flops | bytes accessed | tf_op | source)
XLA Modules:
  0.0 117.4 jit_solution(14311266621675212641)
XLA Ops:
  0.6 1.3 %reshape.10.gain1_ref = f32[1,768]{1,0:T(1,128)} reshape(f32[768]{0:T(1024)} %param.12) | data formatting | bytes 6144 | tf_op jit(solution)/shard_map/reshape | solution.py:457
  1.9 1.3 %reshape.11.gain2_ref = f32[1,768]{1,0:T(1,128)} reshape(f32[768]{0:T(1024)} %param.15) | data formatting | bytes 6144 | tf_op jit(solution)/shard_map/reshape | solution.py:458
  3.2 1.5 %copy.11.dest_ref = s32[512,1]{1,0:T(8,128)} copy(s32[512,1]{0,1:T(1,128)} %param.10) | data formatting | bytes 4096 | tf_op args[1]
  4.7 109.0 %shard_map.104 = (bf16[512,768]{1,0:T(8,128)(2,1)}, f32[16,16,48]{2,1,0:T(8,128)}) custom-call(bf16[512,1536]{1,0:T(8,128)(2,1)} %feats_hbm.1, s32[512,1]{1,0:T(8,128)} %copy.11.dest_ref, bf16[1536,768]{1,0:T(8,128)(2,1)} %embed_hbm.1, f32[1,768]{1,0:T(1,128)} %reshape.10.gain1_ref, bf16[768,2304]{1,0:T(8,128)(2,1)} %qkv_hbm.1, bf16[768,768]{1,0:T(8,128)(2,1)} %out_hbm.1, ...), custom_call_target="tpu_custom_call" | custom-call | tf_op jit(solution)/shard_map/pallas_call | solution.py:406
  113.8 2.1 %copy.14 = bf16[512,768]{1,0:T(8,128)(2,1)} copy(bf16[512,768]{1,0:T(8,128)(2,1)} %get-tuple-element.8) | data formatting | bytes 1572864
  115.8 1.6 %copy.15 = f32[1,16,16,48]{3,2,1,0:T(8,128)} copy(f32[1,16,16,48]{3,2,1,0:T(8,128)} %bitcast.1) | data formatting | bytes 98304
where the time goes:
time: 118 us; the launch traced here: 117 us
  Pallas kernels  109 us (92%)
  local copies, waits for them, and re-layouts  7.7 us (7%)
    pallas_call x1, Pallas kernels, on_device(): pl.pallas_call(kernel, out_shape=(jax.ShapeDtypeStruct((TILES, D), BF16),...  109 us
    unnamed x3, local copies, waits for them, and re-layouts  5.16 us

commit v1 on v0

--- a/solution.py
+++ b/solution.py
@@ -71,17 +71,38 @@
     q_t, k_ref, v_t, scores, near, peak, mixed,
     far_send, far_recv, res_send, res_recv, far_t,
     send2, recv2, hidden, total,
-    load_sem, send1_sem, recv1_sem, fsend_sem, frecv_sem, rsend_sem, rrecv_sem, send2_sem, recv2_sem,
+    load_sem, send1_sem, recv1_sem, fsend_sem, frecv_sem, rsend_sem, rrecv_sem, send2_sem, recv2_sem, keep_sem,
 ):
     dp, sq = lax.axis_index("dp"), lax.axis_index("seq")
     me = dp * N_SEQ + sq
 
-    def partner(k):
-        k = (k * 37) % DEVICES
-        x = (dp + k // 32) % 4
-        z = (sq // 8 + (k // 8) % 4) % 4
-        y = (sq // 2 + (k // 2) % 4) % 4
-        return x, z * 8 + y * 2 + (sq + k) % 2
+    x0, z0, y0, c0 = dp, sq // 8, lax.rem(sq // 2, 4), lax.rem(sq, 2)
+    x_up = [lax.rem(x0 + i, 4) for i in range(4)]
+    x_down = [lax.rem(x0 + 4 - i, 4) for i in range(4)]
+    z_up = [lax.rem(z0 + i, 4) for i in range(4)]
+    place = lax.rem(sq, 8)
+    places = [lax.rem(y0 + i // 2, 4) * 2 + lax.rem(c0 + i, 2) for i in range(8)]
+
+    def each_partner(t, forward, act, skip_self):
+        for i in range(4):
+            turn = lax.rem(i + t + 1, 4)
+            x = x_up[i] if forward else x_down[i]
+            z = lax.rem(z0 + turn, 4) if forward else lax.rem(z0 + 4 - turn, 4)
+            for j in range(8):
+                if not (skip_self and i == 0 and j == 0):
+                    act(4 * t + i, x, z * 8 + places[j], places[j])
+
+    def all_partners(forward, act):
+        def some(t, carry):
+            each_partner(t, forward, act, False)
+            return carry
+
+        lax.fori_loop(0, 3, some, 0)
+        each_partner(3, forward, act, True)
+
+    def unit_of(j):
+        i = (x0 + 4 - (j >> 2)) & 3
+        return (((z0 - (j & 3) + 8 - i - 1) & 3) << 2) + i
 
     loads = [
         pltpu.make_async_copy(src, dst, load_sem.at[i])
@@ -94,20 +115,18 @@
 
     barrier = pltpu.get_barrier_semaphore()
 
-    def greet(k, carry):
-        x, s = partner(k)
+    def greet(unit, x, s, p):
         pl.semaphore_signal(barrier, inc=1, device_id=(x, s), device_id_type=MESH)
-        return carry
-
-    lax.fori_loop(1, DEVICES, greet, 0)
+
+    all_partners(True, greet)
 
     dest = dest_ref[...]
-    onehot = (dest == iota((TILES, DEVICES), 1)).astype(F32)
-    below = (iota((TILES, TILES), 1) < iota((TILES, TILES), 0)).astype(BF16)
-    rank = jnp.sum(dot(below, onehot.astype(BF16)) * onehot, axis=1, keepdims=True)
+    onehot = (dest == iota((DEVICES, TILES), 0)).astype(F32)
+    before = (iota((TILES, TILES), 0) < iota((TILES, TILES), 1)).astype(BF16)
+    rank = jnp.sum(dot(onehot.astype(BF16), before) * onehot, axis=0, keepdims=True)
     slots = dest.astype(F32) * CAP + rank
-    slot_col[...] = jnp.broadcast_to(slots, (TILES, 128))
-    slot_row = jnp.transpose(slot_col[...])[0:1, :].astype(jnp.int32)
+    slot_col[...] = jnp.transpose(jnp.broadcast_to(slots, (128, TILES)))
+    slot_row = slots.astype(jnp.int32)
 
     loads[0].wait()
     loads[1].wait()
@@ -115,12 +134,12 @@
         rows = pl.ds(i * 128, 128)
         tile_rows = dot(feats[rows, :], embed_w[...]).astype(BF16)
         embedded[rows, :] = tile_rows
-        normed[rows, :] = layer_norm(tile_rows.astype(F32), gain1_ref[...])
+        normed[rows, :] = layer_norm(tile_rows.astype(F32), gain1_ref[...].reshape(1, D))
 
     def pack(i, carry):
-        place = (iota((256, TILES), 0) + i * 256 == slot_row).astype(F32)
-        rows = dot(place.astype(BF16), normed[...])
-        used = jnp.sum(place, axis=1, keepdims=True)
+        chosen = (iota((256, TILES), 0) + i * 256 == slot_row).astype(F32)
+        rows = dot(chosen.astype(BF16), normed[...])
+        used = jnp.sum(chosen, axis=1, keepdims=True)
         first = jnp.where((iota((256, 128), 1) == 0) & (used < 0.5), EMPTY, rows[:, :128])
         send1[pl.ds(i * 32, 32)] = to_message(jnp.concatenate([first, rows[:, 128:]], axis=1))
         return carry
@@ -128,16 +147,14 @@
     lax.fori_loop(0, 4, pack, 0)
     pl.semaphore_wait(barrier, DEVICES - 1)
 
-    def send_rows(k, carry):
-        x, s = partner(k)
+    def send_rows(unit, x, s, p):
         pltpu.make_async_remote_copy(
-            src_ref=send1.at[x * N_SEQ + s], dst_ref=recv1.at[me], send_sem=send1_sem, recv_sem=recv1_sem.at[me],
-            device_id=(x, s), device_id_type=MESH,
+            src_ref=send1.at[x * N_SEQ + s], dst_ref=recv1.at[unit * 8 + place], send_sem=send1_sem,
+            recv_sem=recv1_sem.at[unit // 4], device_id=(x, s), device_id_type=MESH,
         ).start()
-        return carry
-
-    lax.fori_loop(1, DEVICES, send_rows, 0)
-    pltpu.make_async_copy(send1.at[me], recv1.at[me], recv1_sem.at[me]).start()
+
+    all_partners(True, send_rows)
+    pltpu.make_async_copy(send1.at[me], recv1.at[12 * 8 + place], recv1_sem.at[3]).start()
 
     loads[2].wait()
 
@@ -154,13 +171,9 @@
         q_t[h, pl.ds(base + HEAD, 16), :] = one_row
         v_t[h, pl.ds(HEAD, 16), :] = jnp.ones((16, SLOTS), BF16)
 
-    def arrived1(s, carry):
-        pltpu.make_async_copy(send1.at[s], recv1.at[s], recv1_sem.at[s]).wait()
-        return carry
-
-    lax.fori_loop(0, DEVICES, arrived1, 0)
-
     def project(g, carry):
+        group = recv1.at[pl.ds(g * 32, 32)]
+        pltpu.make_async_copy(group, group, recv1_sem.at[g]).wait()
         rows = from_message(recv1[pl.ds(g * 32, 32)])
         empty = rows[:, 0:1] > 0.1 * EMPTY
         rows = jnp.where(empty, 0.0, rows).astype(BF16)
@@ -186,7 +199,8 @@
     lax.fori_loop(0, 4, project, 0)
 
     rows = x_ref[:, pl.ds(0, 16), :].reshape(256, D)
-    swap = (iota((256, 256), 1) == (iota((256, 256), 0) & 15) * 16 + (iota((256, 256), 0) >> 4)).astype(BF16)
+    row = iota((256, 256), 0)
+    swap = (iota((256, 256), 1) == unit_of(row & 15) * 16 + (row >> 4)).astype(BF16)
     rows = dot(swap, rows).astype(BF16)
     bias = dot(swap, bias_ref[:, pl.ds(0, 16), :].reshape(256, 128))
     low = HEAD * (iota((256, D), 0) >> 4)
@@ -212,21 +226,24 @@
         [far_q.reshape(HEADS, ROWS, 128), far_kv.reshape(HEADS, ROWS, 128)], axis=1
     ).astype(BF16)
 
-    def send_far(h, carry):
-        @pl.when(2 * h != sq)
-        def _():
-            pltpu.make_async_remote_copy(
-                src_ref=far_send.at[h], dst_ref=far_recv.at[sq], send_sem=fsend_sem, recv_sem=frecv_sem.at[sq],
-                device_id=(dp, 2 * h), device_id_type=MESH,
-            ).start()
-
-        @pl.when(2 * h == sq)
-        def _():
-            pltpu.make_async_copy(far_send.at[h], far_recv.at[sq], frecv_sem.at[sq]).start()
-
-        return carry
-
-    lax.fori_loop(0, HEADS, send_far, 0)
+    mine = sq // 2
+    for i in range(1, HEADS):
+        h = lax.rem(mine + i, HEADS)
+        pltpu.make_async_remote_copy(
+            src_ref=far_send.at[h], dst_ref=far_recv.at[sq], send_sem=fsend_sem, recv_sem=frecv_sem.at[sq],
+            device_id=(dp, 2 * h), device_id_type=MESH,
+        ).start()
+
+    @pl.when(c0 == 1)
+    def _():
+        pltpu.make_async_remote_copy(
+            src_ref=far_send.at[mine], dst_ref=far_recv.at[sq], send_sem=fsend_sem, recv_sem=frecv_sem.at[sq],
+            device_id=(dp, 2 * mine), device_id_type=MESH,
+        ).start()
+
+    @pl.when(c0 == 0)
+    def _():
+        pltpu.make_async_copy(far_send.at[mine], far_recv.at[sq], frecv_sem.at[sq]).start()
 
     parts = SLOTS // QUERIES
 
@@ -235,24 +252,36 @@
             k_ref[h // 2], q_t[h, :, i * QUERIES : (i + 1) * QUERIES], (((1,), (0,)), ((), ())), preferred_element_type=F32
         )
 
+    def attend_head(h, act=None):
+        for i in range(parts):
+            if i + 1 < parts:
+                later = score(h, i + 1)
+            else:
+                later = score(jnp.minimum(h + 1, HEADS - 1), 0)
+            if act is not None and i == 0:
+                act()
+            block = scores[i % 2]
+            top = jnp.max(block, axis=0, keepdims=True)
+            weights = jnp.exp2(block - top).astype(BF16)
+            near[h, :, i * QUERIES : (i + 1) * QUERIES] = dot(v_t[h], weights)
+            peak[h, :, i * QUERIES : (i + 1) * QUERIES] = jnp.broadcast_to(top, (8, QUERIES))
+            scores[(i + 1) % 2] = later
+
     def attend(first, last):
-        scores[0] = score(first, 0)
-
         def one_head(h, carry):
-            for i in range(parts):
-                if i + 1 < parts:
-                    later = score(h, i + 1)
-                else:
-                    later = score(jnp.minimum(h + 1, last - 1), 0)
-                block = scores[i % 2]
-                top = jnp.max(block, axis=0, keepdims=True)
-                weights = jnp.exp2(block - top).astype(BF16)
-                near[h, :, i * QUERIES : (i + 1) * QUERIES] = dot(v_t[h], weights)
-                peak[h, :, i * QUERIES : (i + 1) * QUERIES] = jnp.broadcast_to(top, (8, QUERIES))
-                scores[(i + 1) % 2] = later
+            attend_head(h)
             return carry
 
         lax.fori_loop(first, last, one_head, 0)
+
+    def attend_and_send(first, c):
+        def one_head(t, carry):
+            attend_head(first + t, lambda: each_partner(t, False, send_back(c), False))
+            return carry
+
+        lax.fori_loop(0, 3, one_head, 0)
+        attend_head(first + 3, lambda: each_partner(3, False, send_back(c), True))
+        attend_head(first + 4)
 
     def far_branch():
         def arrived(s, carry):
@@ -268,20 +297,14 @@
         summed = result[:, 64 + HEAD : 65 + HEAD]
         result = jnp.where(iota(result.shape, 1) < 64, top + jnp.log2(summed), result / summed)
         res_send[...] = result.reshape(N_SEQ, ROWS, 128)
-        head = sq // 2
-
-        def answer(s, carry):
-            @pl.when(s != sq)
-            def _():
-                pltpu.make_async_remote_copy(
-                    src_ref=res_send.at[s], dst_ref=res_recv.at[head], send_sem=rsend_sem, recv_sem=rrecv_sem.at[head],
-                    device_id=(dp, s), device_id_type=MESH,
-                ).start()
-
-            return carry
-
-        lax.fori_loop(0, N_SEQ, answer, 0)
-        pltpu.make_async_copy(res_send.at[sq], res_recv.at[head], rrecv_sem.at[head]).start()
+
+        for i in range(1, N_SEQ):
+            s = lax.rem(sq + i, N_SEQ)
+            pltpu.make_async_remote_copy(
+                src_ref=res_send.at[s], dst_ref=res_recv.at[mine], send_sem=rsend_sem, recv_sem=rrecv_sem.at[mine],
+                device_id=(dp, s), device_id_type=MESH,
+            ).start()
+        pltpu.make_async_copy(res_send.at[sq], res_recv.at[mine], rrecv_sem.at[mine]).start()
         pltpu.make_async_copy(
             res_send.at[pl.ds(0, N_SEQ - 1)], res_send.at[pl.ds(0, N_SEQ - 1)], rsend_sem
         ).wait()
@@ -300,7 +323,7 @@
         lowest = results - high - middle
         split = jnp.where(lane >= 64, results, jnp.where(lane == 0, high, jnp.where(lane == 1, middle, lowest)))
         row = iota((HEADS * ROWS, SLOTS), 0)
-        spread = (iota((HEADS * ROWS, SLOTS), 1) == (row & 15) * RATE + (row >> 4)).astype(BF16)
+        spread = (iota((HEADS * ROWS, SLOTS), 1) == unit_of(row & 15) * RATE + (row >> 4)).astype(BF16)
         far_t[...] = lax.dot_general(split.astype(BF16), spread, TN, preferred_element_type=F32)
 
     def blend(first, last):
@@ -319,60 +342,59 @@
 
         lax.fori_loop(first, last, one_head, 0)
 
-    def give_back(c):
-        def pack_back(g, carry):
+    def pack_back(c):
+        def some(g, carry):
             lanes = pl.ds(pl.multiple_of(g * 256, 256), 256)
             rows = jnp.transpose(mixed[256 * c : 256 * (c + 1), lanes].astype(F32))
             send2[c, pl.ds(g * 32, 32)] = to_message(rows)
             return carry
 
-        lax.fori_loop(0, 4, pack_back, 0)
-
-        def send_back(k, carry):
-            x, s = partner(k)
+        lax.fori_loop(0, 4, some, 0)
+        pltpu.make_async_copy(send2.at[c, 12 * 8 + place], recv2.at[c, me], keep_sem.at[c]).start()
+
+    def send_back(c):
+        def act(unit, x, s, p):
             pltpu.make_async_remote_copy(
-                src_ref=send2.at[c, x * N_SEQ + s], dst_ref=recv2.at[c, me], send_sem=send2_sem.at[c], recv_sem=recv2_sem.at[c, me],
-                device_id=(x, s), device_id_type=MESH,
+                src_ref=send2.at[c, unit * 8 + p], dst_ref=recv2.at[c, me], send_sem=send2_sem.at[c],
+                recv_sem=recv2_sem.at[c], device_id=(x, s), device_id_type=MESH,
             ).start()
-            return carry
-
-        lax.fori_loop(1, DEVICES, send_back, 0)
-        pltpu.make_async_copy(send2.at[c, me], recv2.at[c, me], recv2_sem.at[c, me]).start()
-
+
+        return act
+
+    scores[0] = score(0, 0)
     attend(0, 3)
 
-    @pl.when(sq % 2 == 0)
+    @pl.when(c0 == 0)
     def _():
         far_branch()
 
     attend(3, 6)
     far_arrived()
     blend(0, 6)
-    give_back(0)
-    attend(6, 11)
+    pack_back(0)
+    attend_and_send(6, 0)
     blend(6, 11)
-    give_back(1)
-    attend(11, 16)
+    pack_back(1)
+    attend_and_send(11, 1)
     blend(11, 16)
-    give_back(2)
+    pack_back(2)
+    all_partners(False, send_back(2))
 
     loads[3].wait()
     hidden[...] = embedded[...].astype(F32)
     for c in range(3):
-        def arrived2(s, carry, c=c):
-            pltpu.make_async_copy(send2.at[c, s], recv2.at[c, s], recv2_sem.at[c, s]).wait()
-            return carry
-
-        lax.fori_loop(0, DEVICES, arrived2, 0)
+        pltpu.make_async_copy(send2.at[c, 12 * 8 + place], recv2.at[c, me], keep_sem.at[c]).wait()
+        most = recv2.at[c, pl.ds(0, DEVICES - 1)]
+        pltpu.make_async_copy(most, most, recv2_sem.at[c]).wait()
         taken = jnp.zeros((TILES, 256), F32)
         for g in range(4):
-            place = (iota((TILES, 256), 1) + g * 256 == slot_col[:, 0:1].astype(jnp.int32)).astype(BF16)
-            taken = taken + dot(place, from_message(recv2[c, pl.ds(g * 32, 32)]).astype(BF16))
+            chosen = (iota((TILES, 256), 1) + g * 256 == slot_col[:, 0:1].astype(jnp.int32)).astype(BF16)
+            taken = taken + dot(chosen, from_message(recv2[c, pl.ds(g * 32, 32)]).astype(BF16))
         hidden[...] += dot(taken.astype(BF16), out_w[256 * c : 256 * (c + 1), :])
     loads[4].wait()
     loads[5].wait()
     state = hidden[...].astype(BF16).astype(F32)
-    normed[...] = layer_norm(state, gain2_ref[...])
+    normed[...] = layer_norm(state, gain2_ref[...].reshape(1, D))
     total[...] = state
 
     def feed(i, carry):
@@ -390,11 +412,11 @@
     for c in range(3):
         pltpu.make_async_copy(send2.at[c, most], send2.at[c, most], send2_sem.at[c]).wait()
 
-    @pl.when(sq % 2 == 0)
+    @pl.when(c0 == 0)
     def _():
         pltpu.make_async_copy(far_send.at[pl.ds(0, 15)], far_send.at[pl.ds(0, 15)], fsend_sem).wait()
 
-    @pl.when(sq % 2 == 1)
+    @pl.when(c0 == 1)
     def _():
         pltpu.make_async_copy(far_send, far_send, fsend_sem).wait()
 
@@ -444,18 +466,19 @@
             pltpu.VMEM((TILES, D), F32),
             dma((6,)),
             dma,
-            dma((DEVICES,)),
+            dma((4,)),
             dma,
             dma((N_SEQ,)),
             dma,
             dma((HEADS,)),
             dma((3,)),
-            dma((3, DEVICES)),
+            dma((3,)),
+            dma((3,)),
         ],
         compiler_params=pltpu.CompilerParams(collective_id=0, has_side_effects=True, vmem_limit_bytes=62 << 20),
     )(
-        tile_feats, tile_dest, embed_weight, norm1_gain.reshape(1, D), qkv_weight, out_weight,
-        norm2_gain.reshape(1, D), up_weight, down_weight,
+        tile_feats, tile_dest.reshape(1, TILES), embed_weight, norm1_gain, qkv_weight, out_weight,
+        norm2_gain, up_weight, down_weight,
     )
     return tile_out, far_heads[None]
 

time: 118 us -> 88.5 us (0.75)
  Pallas kernels: 109 us -> 84.1 us
  local copies, waits for them, and re-layouts: 7.7 us -> 3.63 us
    pallas_call x1, Pallas kernels: 109 us -> 84.1 us  [on_device(): pl.pallas_call(kernel, out_shape=(jax.ShapeDtypeStruct((TILES, D), BF16),...]
    reshape x2 -> x0, local copies, waits for them, and re-layouts: 2.54 us -> none  [the longest x1 1.27 us: on_device(): norm2_gain.reshape(1, D)]
    unnamed x3 -> x2, local copies, waits for them, and re-layouts: 5.16 us -> 3.63 us
where the time goes in v1:
time: 88.5 us; the launch traced here: 88.4 us
  Pallas kernels  84.1 us (95%)
  local copies, waits for them, and re-layouts  3.63 us (4%)
    pallas_call x1, Pallas kernels, on_device(): pl.pallas_call(kernel, out_shape=(jax.ShapeDtypeStruct((TILES, D), BF16),...  84.1 us
    unnamed x2, local copies, waits for them, and re-layouts  3.63 us

profile of v1, /device:TPU:1, one launch (start us, length us, event | category | flops | bytes accessed | tf_op | source)
XLA Modules:
  0.0 88.4 jit_solution(12907041097475077548)
XLA Ops:
  0.6 84.1 %shard_map.104 = (bf16[512,768]{1,0:T(8,128)(2,1)}, f32[16,16,48]{2,1,0:T(8,128)}) custom-call(bf16[512,1536]{1,0:T(8,128)(2,1)} %feats_hbm.1, s32[1,512]{1,0:T(1,128)} %bitcast.3, bf16[1536,768]{1,0:T(8,128)(2,1)} %embed_hbm.1, f32[768]{0:T(1024)} %gain1_ref.1, bf16[768,2304]{1,0:T(8,128)(2,1)} %qkv_hbm.1, bf16[768,768]{1,0:T(8,128)(2,1)} %out_hbm.1, ...), custom_call_target="tpu_custom_call" | custom-call | tf_op jit(solution)/shard_map/pallas_call | solution.py:428
  84.7 2.1 %copy.13 = bf16[512,768]{1,0:T(8,128)(2,1)} copy(bf16[512,768]{1,0:T(8,128)(2,1)} %get-tuple-element.8) | data formatting | bytes 1572864
  86.8 1.6 %copy.14 = f32[1,16,16,48]{3,2,1,0:T(8,128)} copy(f32[1,16,16,48]{3,2,1,0:T(8,128)} %bitcast.2) | data formatting | bytes 98304

commit v2 on v1

--- a/solution.py
+++ b/solution.py
@@ -67,9 +67,9 @@
     feats_hbm, dest_ref, embed_hbm, gain1_ref, qkv_hbm, out_hbm, gain2_ref, up_hbm, down_hbm,
     tile_ref, far_ref,
     feats, embed_w, qkv_w, out_w, up_w, down_w, qkv_t,
-    embedded, normed, slot_col, send1, recv1, x_ref, bias_ref,
+    embedded, normed, slot_col, send1, recv1,
     q_t, k_ref, v_t, scores, near, peak, mixed,
-    far_send, far_recv, res_send, res_recv, far_t,
+    far_cols, far_send, far_recv, res_send, res_recv, far_t,
     send2, recv2, hidden, total,
     load_sem, send1_sem, recv1_sem, fsend_sem, frecv_sem, rsend_sem, rrecv_sem, send2_sem, recv2_sem, keep_sem,
 ):
@@ -178,8 +178,6 @@
         empty = rows[:, 0:1] > 0.1 * EMPTY
         rows = jnp.where(empty, 0.0, rows).astype(BF16)
         bias = jnp.broadcast_to(jnp.where(empty, MASKED, 0.0), (256, 128))
-        x_ref[pl.ds(g * 4, 4)] = rows.reshape(4, RATE, D)
-        bias_ref[pl.ds(g * 4, 4)] = bias.astype(BF16).reshape(4, RATE, 128)
         lanes = pl.ds(pl.multiple_of(g * 256, 256), 256)
         query = (lax.dot_general(qkv_t[0:D, :], rows, NT, preferred_element_type=F32) * SCALE).astype(BF16)
         for h in range(HEADS):
@@ -194,56 +192,45 @@
         value = lax.dot_general(qkv_t[2 * D :, :], rows, NT, preferred_element_type=F32).astype(BF16)
         for h in range(HEADS):
             v_t[h, pl.ds(0, HEAD), lanes] = value[h * HEAD : (h + 1) * HEAD]
+        lane, column = iota((256, 256), 0), iota((256, 256), 1)
+        taken = ((lane & (RATE - 1)) == (column >> 4)) & (g * 4 + (lane >> 6) == unit_of(column & 15))
+        taken = taken.astype(BF16)
+        owner = iota((HEAD, 256), 1) >> 4
+        for n, part in enumerate((query, key.astype(BF16), value)):
+            wide = dot(part, taken)
+            own = jnp.zeros((HEAD, 256), F32)
+            for h in range(HEADS):
+                own = own + jnp.where(owner == h, wide[h * HEAD : (h + 1) * HEAD], 0.0)
+            far_cols[n * HEAD : (n + 1) * HEAD, :] += own
+        far_cols[3 * HEAD :, :] += dot(masks.astype(BF16), taken)
         return carry
 
+    far_cols[...] = jnp.zeros_like(far_cols)
     lax.fori_loop(0, 4, project, 0)
 
-    rows = x_ref[:, pl.ds(0, 16), :].reshape(256, D)
-    row = iota((256, 256), 0)
-    swap = (iota((256, 256), 1) == unit_of(row & 15) * 16 + (row >> 4)).astype(BF16)
-    rows = dot(swap, rows).astype(BF16)
-    bias = dot(swap, bias_ref[:, pl.ds(0, 16), :].reshape(256, 128))
-    low = HEAD * (iota((256, D), 0) >> 4)
-    column = iota((256, D), 1)
-    own = (column >= low) & (column < low + HEAD)
-    turns = (iota((D, 128), 0) - iota((D, 128), 1)).astype(F32) * (1.0 / HEAD)
-    whole = jnp.abs(turns - jnp.round(turns)) < 0.01
-    lane = iota((D, 128), 1)
-    to_front = (whole & (lane < HEAD)).astype(BF16)
-    turns = turns + (64.0 / HEAD)
-    whole = jnp.abs(turns - jnp.round(turns)) < 0.01
-    to_back = (whole & (lane >= 64) & (lane < 64 + HEAD)).astype(BF16)
-
-    def own_head(part, scale):
-        product = dot(rows, qkv_w[:, part * D : (part + 1) * D]) * scale
-        return jnp.where(own, product, 0.0).astype(BF16)
-
-    lane = iota((256, 128), 1)
-    far_q = jnp.where(lane == HEAD, 1.0, dot(own_head(0, SCALE), to_front))
-    far_kv = dot(own_head(1, 1.0), to_front) + dot(own_head(2, 1.0), to_back)
-    far_kv = jnp.where(lane == HEAD, bias, jnp.where(lane == 64 + HEAD, 1.0, far_kv))
+    one = jnp.where(iota((16, 256), 0) == 0, 1.0, 0.0)
+    far_q = jnp.concatenate([far_cols[0:HEAD, :], one, jnp.zeros((64, 256), F32)], axis=0)
+    far_kv = jnp.concatenate(
+        [far_cols[HEAD : 2 * HEAD, :], far_cols[3 * HEAD :, :], far_cols[2 * HEAD : 3 * HEAD, :], one], axis=0
+    )
     far_send[...] = jnp.concatenate(
-        [far_q.reshape(HEADS, ROWS, 128), far_kv.reshape(HEADS, ROWS, 128)], axis=1
+        [jnp.transpose(far_q).reshape(HEADS, ROWS, 128), jnp.transpose(far_kv).reshape(HEADS, ROWS, 128)], axis=1
     ).astype(BF16)
 
     mine = sq // 2
+
+    def send_far(h, s):
+        pltpu.make_async_remote_copy(
+            src_ref=far_send.at[h], dst_ref=far_recv.at[sq], send_sem=fsend_sem, recv_sem=frecv_sem,
+            device_id=(dp, s), device_id_type=MESH,
+        ).start()
+
     for i in range(1, HEADS):
         h = lax.rem(mine + i, HEADS)
-        pltpu.make_async_remote_copy(
-            src_ref=far_send.at[h], dst_ref=far_recv.at[sq], send_sem=fsend_sem, recv_sem=frecv_sem.at[sq],
-            device_id=(dp, 2 * h), device_id_type=MESH,
-        ).start()
-
-    @pl.when(c0 == 1)
-    def _():
-        pltpu.make_async_remote_copy(
-            src_ref=far_send.at[mine], dst_ref=far_recv.at[sq], send_sem=fsend_sem, recv_sem=frecv_sem.at[sq],
-            device_id=(dp, 2 * mine), device_id_type=MESH,
-        ).start()
-
-    @pl.when(c0 == 0)
-    def _():
-        pltpu.make_async_copy(far_send.at[mine], far_recv.at[sq], frecv_sem.at[sq]).start()
+        send_far(h, 2 * h)
+        send_far(h, 2 * h + 1)
+    send_far(mine, 2 * mine + 1 - c0)
+    pltpu.make_async_copy(far_send.at[mine], far_recv.at[sq], frecv_sem).start()
 
     parts = SLOTS // QUERIES
 
@@ -257,7 +244,7 @@
             if i + 1 < parts:
                 later = score(h, i + 1)
             else:
-                later = score(jnp.minimum(h + 1, HEADS - 1), 0)
+                later = score(jnp.minimum(h + 1, HEADS - 1) if not isinstance(h, int) else min(h + 1, HEADS - 1), 0)
             if act is not None and i == 0:
                 act()
             block = scores[i % 2]
@@ -268,11 +255,8 @@
             scores[(i + 1) % 2] = later
 
     def attend(first, last):
-        def one_head(h, carry):
+        for h in range(first, last):
             attend_head(h)
-            return carry
-
-        lax.fori_loop(first, last, one_head, 0)
 
     def attend_and_send(first, c):
         def one_head(t, carry):
@@ -284,37 +268,37 @@
         attend_head(first + 4)
 
     def far_branch():
-        def arrived(s, carry):
-            pltpu.make_async_copy(far_recv.at[s], far_recv.at[s], frecv_sem.at[s]).wait()
-            return carry
-
-        lax.fori_loop(0, N_SEQ, arrived, 0)
-        queries = far_recv[:, pl.ds(0, 16), :].reshape(N_SEQ * ROWS, 128)
+        pltpu.make_async_copy(far_recv, far_recv, frecv_sem).wait()
+        half = N_SEQ // 2
+        queries = far_recv[pl.ds(half * c0, half), pl.ds(0, 16), :].reshape(half * ROWS, 128)
         pairs = far_recv[:, pl.ds(16, 16), :].reshape(N_SEQ * ROWS, 128)
         block = lax.dot_general(queries, pairs, NT, preferred_element_type=F32)
         top = jnp.max(block, axis=1, keepdims=True)
         result = dot(jnp.exp2(block - top).astype(BF16), pairs)
         summed = result[:, 64 + HEAD : 65 + HEAD]
         result = jnp.where(iota(result.shape, 1) < 64, top + jnp.log2(summed), result / summed)
-        res_send[...] = result.reshape(N_SEQ, ROWS, 128)
-
-        for i in range(1, N_SEQ):
-            s = lax.rem(sq + i, N_SEQ)
+        res_send[...] = result.reshape(half, ROWS, 128)
+
+        def answer(i):
+            to = lax.rem(sq + i, half)
             pltpu.make_async_remote_copy(
-                src_ref=res_send.at[s], dst_ref=res_recv.at[mine], send_sem=rsend_sem, recv_sem=rrecv_sem.at[mine],
-                device_id=(dp, s), device_id_type=MESH,
+                src_ref=res_send.at[to], dst_ref=res_recv.at[mine], send_sem=rsend_sem, recv_sem=rrecv_sem,
+                device_id=(dp, half * c0 + to), device_id_type=MESH,
             ).start()
-        pltpu.make_async_copy(res_send.at[sq], res_recv.at[mine], rrecv_sem.at[mine]).start()
-        pltpu.make_async_copy(
-            res_send.at[pl.ds(0, N_SEQ - 1)], res_send.at[pl.ds(0, N_SEQ - 1)], rsend_sem
-        ).wait()
+
+        for i in range(1, half):
+            answer(i)
+
+        @pl.when(sq // half != c0)
+        def _():
+            answer(0)
+
+        @pl.when(sq // half == c0)
+        def _():
+            pltpu.make_async_copy(res_send.at[lax.rem(sq, half)], res_recv.at[mine], rrecv_sem).start()
 
     def far_arrived():
-        def arrived(h, carry):
-            pltpu.make_async_copy(res_recv.at[h], res_recv.at[h], rrecv_sem.at[h]).wait()
-            return carry
-
-        lax.fori_loop(0, HEADS, arrived, 0)
+        pltpu.make_async_copy(res_recv, res_recv, rrecv_sem).wait()
         results = res_recv[...].reshape(HEADS * ROWS, 128)
         far_ref[...] = res_recv[:, :, 64 : 64 + HEAD]
         lane = iota((HEADS * ROWS, 128), 1)
@@ -363,11 +347,7 @@
 
     scores[0] = score(0, 0)
     attend(0, 3)
-
-    @pl.when(c0 == 0)
-    def _():
-        far_branch()
-
+    far_branch()
     attend(3, 6)
     far_arrived()
     blend(0, 6)
@@ -397,14 +377,26 @@
     normed[...] = layer_norm(state, gain2_ref[...].reshape(1, D))
     total[...] = state
 
-    def feed(i, carry):
-        columns = pl.ds(pl.multiple_of(i * FF_BLOCK, FF_BLOCK), FF_BLOCK)
-        inner = dot(normed[...], up_w[:, columns])
-        inner = jax.nn.gelu(inner, approximate=True).astype(BF16)
-        total[...] += dot(inner, down_w[columns, :])
+    def columns(i):
+        return pl.ds(i * FF_BLOCK if isinstance(i, int) else pl.multiple_of(i * FF_BLOCK, FF_BLOCK), FF_BLOCK)
+
+    def feed(i, slot, last):
+        if not last:
+            later = dot(normed[...], up_w[:, columns(i + 1)])
+        inner = jax.nn.gelu(scores[slot, 0:TILES, :], approximate=True).astype(BF16)
+        total[...] += dot(inner, down_w[columns(i), :])
+        if not last:
+            scores[1 - slot, 0:TILES, :] = later
+
+    def feed_two(k, carry):
+        feed(2 * k, 0, False)
+        feed(2 * k + 1, 1, False)
         return carry
 
-    lax.fori_loop(0, FF // FF_BLOCK, feed, 0)
+    scores[0, 0:TILES, :] = dot(normed[...], up_w[:, columns(0)])
+    lax.fori_loop(0, FF // FF_BLOCK // 2 - 1, feed_two, 0)
+    feed(FF // FF_BLOCK - 2, 0, False)
+    feed(FF // FF_BLOCK - 1, 1, True)
     tile_ref[...] = total[...].astype(BF16)
 
     most = pl.ds(0, DEVICES - 1)
@@ -412,13 +404,17 @@
     for c in range(3):
         pltpu.make_async_copy(send2.at[c, most], send2.at[c, most], send2_sem.at[c]).wait()
 
-    @pl.when(c0 == 0)
+    most = far_recv.at[pl.ds(0, N_SEQ - 1)]
+    pltpu.make_async_copy(most, most, fsend_sem).wait()
+
+    @pl.when(sq // 16 == c0)
     def _():
-        pltpu.make_async_copy(far_send.at[pl.ds(0, 15)], far_send.at[pl.ds(0, 15)], fsend_sem).wait()
-
-    @pl.when(c0 == 1)
+        most = res_send.at[pl.ds(0, 15)]
+        pltpu.make_async_copy(most, most, rsend_sem).wait()
+
+    @pl.when(sq // 16 != c0)
     def _():
-        pltpu.make_async_copy(far_send, far_send, fsend_sem).wait()
+        pltpu.make_async_copy(res_send, res_send, rsend_sem).wait()
 
 
 def on_device(tile_feats, tile_dest, embed_weight, norm1_gain, qkv_weight, out_weight, norm2_gain, up_weight, down_weight):
@@ -446,8 +442,6 @@
             pltpu.VMEM((TILES, 128), F32),
             pltpu.VMEM((DEVICES, 16, 384), BF16),
             pltpu.VMEM((DEVICES, 16, 384), BF16),
-            pltpu.VMEM((ROWS, RATE, D), BF16),
-            pltpu.VMEM((ROWS, RATE, 128), BF16),
             pltpu.VMEM((HEADS, 128, SLOTS), BF16),
             pltpu.VMEM((HEADS // 2, SLOTS, 128), BF16),
             pltpu.VMEM((HEADS, 64, SLOTS), BF16),
@@ -455,9 +449,10 @@
             pltpu.VMEM((HEADS, 64, SLOTS), F32),
             pltpu.VMEM((HEADS, 8, SLOTS), F32),
             pltpu.VMEM((D, SLOTS), BF16),
+            pltpu.VMEM((3 * HEAD + 16, 256), F32),
             pltpu.VMEM((HEADS, 32, 128), BF16),
             pltpu.VMEM((N_SEQ, 32, 128), BF16),
-            pltpu.VMEM((N_SEQ, ROWS, 128), F32),
+            pltpu.VMEM((N_SEQ // 2, ROWS, 128), F32),
             pltpu.VMEM((HEADS, ROWS, 128), F32),
             pltpu.VMEM((128, SLOTS), F32),
             pltpu.VMEM((3, DEVICES, 16, 128), BF16),
@@ -468,9 +463,9 @@
             dma,
             dma((4,)),
             dma,
-            dma((N_SEQ,)),
             dma,
-            dma((HEADS,)),
+            dma,
+            dma,
             dma((3,)),
             dma((3,)),
             dma((3,)),

time: 88.5 us -> 85.6 us (0.967)
  Pallas kernels: 84.1 us -> 81.2 us
    pallas_call x1, Pallas kernels: 84.1 us -> 81.2 us  [on_device(): pl.pallas_call(kernel, out_shape=(jax.ShapeDtypeStruct((TILES, D), BF16),...]
where the time goes in v2:
time: 85.6 us; the launch traced here: 85.4 us
  Pallas kernels  81.2 us (95%)
  local copies, waits for them, and re-layouts  3.63 us (4%)
    pallas_call x1, Pallas kernels, on_device(): pl.pallas_call(kernel, out_shape=(jax.ShapeDtypeStruct((TILES, D), BF16),...  81.2 us
    unnamed x2, local copies, waits for them, and re-layouts  3.63 us

profile of v2, /device:TPU:1, one launch (start us, length us, event | category | flops | bytes accessed | tf_op | source)
XLA Modules:
  0.0 85.4 jit_solution(15377703163694851448)
XLA Ops:
  0.6 81.2 %shard_map.104 = (bf16[512,768]{1,0:T(8,128)(2,1)}, f32[16,16,48]{2,1,0:T(8,128)}) custom-call(bf16[512,1536]{1,0:T(8,128)(2,1)} %feats_hbm.1, s32[1,512]{1,0:T(1,128)} %bitcast.3, bf16[1536,768]{1,0:T(8,128)(2,1)} %embed_hbm.1, f32[768]{0:T(1024)} %gain1_ref.1, bf16[768,2304]{1,0:T(8,128)(2,1)} %qkv_hbm.1, bf16[768,768]{1,0:T(8,128)(2,1)} %out_hbm.1, ...), custom_call_target="tpu_custom_call" | custom-call | tf_op jit(solution)/shard_map/pallas_call | solution.py:424
  81.8 2.1 %copy.13 = bf16[512,768]{1,0:T(8,128)(2,1)} copy(bf16[512,768]{1,0:T(8,128)(2,1)} %get-tuple-element.8) | data formatting | bytes 1572864
  83.9 1.6 %copy.14 = f32[1,16,16,48]{3,2,1,0:T(8,128)} copy(f32[1,16,16,48]{3,2,1,0:T(8,128)} %bitcast.2) | data formatting | bytes 98304

commit v3 on v2

--- a/solution.py
+++ b/solution.py
@@ -64,13 +64,13 @@
 
 
 def kernel(
-    feats_hbm, dest_ref, embed_hbm, gain1_ref, qkv_hbm, out_hbm, gain2_ref, up_hbm, down_hbm,
-    tile_ref, far_ref,
-    feats, embed_w, qkv_w, out_w, up_w, down_w, qkv_t,
+    feats_hbm, dest_ref, embed_hbm, gain1_ref, qkv_hbm, out_hbm,
+    state_ref, results_ref,
+    feats, embed_w, qkv_w, out_w, qkv_t,
     embedded, normed, slot_col, send1, recv1,
     q_t, k_ref, v_t, scores, near, peak, mixed,
     far_cols, far_send, far_recv, res_send, res_recv, far_t,
-    send2, recv2, hidden, total,
+    send2, recv2, hidden,
     load_sem, send1_sem, recv1_sem, fsend_sem, frecv_sem, rsend_sem, rrecv_sem, send2_sem, recv2_sem, keep_sem,
 ):
     dp, sq = lax.axis_index("dp"), lax.axis_index("seq")
@@ -107,7 +107,7 @@
     loads = [
         pltpu.make_async_copy(src, dst, load_sem.at[i])
         for i, (src, dst) in enumerate(
-            [(feats_hbm, feats), (embed_hbm, embed_w), (qkv_hbm, qkv_w), (out_hbm, out_w), (up_hbm, up_w), (down_hbm, down_w)]
+            [(feats_hbm, feats), (embed_hbm, embed_w), (qkv_hbm, qkv_w), (out_hbm, out_w)]
         )
     ]
     for load in loads:
@@ -300,7 +300,7 @@
     def far_arrived():
         pltpu.make_async_copy(res_recv, res_recv, rrecv_sem).wait()
         results = res_recv[...].reshape(HEADS * ROWS, 128)
-        far_ref[...] = res_recv[:, :, 64 : 64 + HEAD]
+        results_ref[...] = res_recv[...]
         lane = iota((HEADS * ROWS, 128), 1)
         high = results.astype(BF16).astype(F32)
         middle = (results - high).astype(BF16).astype(F32)
@@ -371,9 +371,45 @@
             chosen = (iota((TILES, 256), 1) + g * 256 == slot_col[:, 0:1].astype(jnp.int32)).astype(BF16)
             taken = taken + dot(chosen, from_message(recv2[c, pl.ds(g * 32, 32)]).astype(BF16))
         hidden[...] += dot(taken.astype(BF16), out_w[256 * c : 256 * (c + 1), :])
-    loads[4].wait()
-    loads[5].wait()
-    state = hidden[...].astype(BF16).astype(F32)
+    state_ref[...] = hidden[...].astype(BF16)
+
+    most = pl.ds(0, DEVICES - 1)
+    pltpu.make_async_copy(send1.at[most], send1.at[most], send1_sem).wait()
+    for c in range(3):
+        pltpu.make_async_copy(send2.at[c, most], send2.at[c, most], send2_sem.at[c]).wait()
+
+    most = far_recv.at[pl.ds(0, N_SEQ - 1)]
+    pltpu.make_async_copy(most, most, fsend_sem).wait()
+
+    @pl.when(sq // 16 == c0)
+    def _():
+        most = res_send.at[pl.ds(0, 15)]
+        pltpu.make_async_copy(most, most, rsend_sem).wait()
+
+    @pl.when(sq // 16 != c0)
+    def _():
+        pltpu.make_async_copy(res_send, res_send, rsend_sem).wait()
+
+
+def feed_kernel(
+    state_ref, results_ref, gain2_ref, up_hbm, down_hbm, tile_ref, far_ref, up_w, down_w, normed, total, scores, load_sem
+):
+    def load(i):
+        part = pl.ds(i * FF_BLOCK if isinstance(i, int) else pl.multiple_of(i * FF_BLOCK, FF_BLOCK), FF_BLOCK)
+        return (
+            pltpu.make_async_copy(up_hbm.at[:, part], up_w.at[:, part], load_sem.at[0, i]),
+            pltpu.make_async_copy(down_hbm.at[part, :], down_w.at[part, :], load_sem.at[1, i]),
+        )
+
+    def arrive(i):
+        for copy in load(i):
+            copy.wait()
+
+    for i in range(FF // FF_BLOCK):
+        for copy in load(i):
+            copy.start()
+    far_ref[...] = results_ref[:, :, 64 : 64 + HEAD]
+    state = state_ref[...].astype(F32)
     normed[...] = layer_norm(state, gain2_ref[...].reshape(1, D))
     total[...] = state
 
@@ -382,60 +418,43 @@
 
     def feed(i, slot, last):
         if not last:
+            arrive(i + 1)
             later = dot(normed[...], up_w[:, columns(i + 1)])
-        inner = jax.nn.gelu(scores[slot, 0:TILES, :], approximate=True).astype(BF16)
+        inner = jax.nn.gelu(scores[slot], approximate=True).astype(BF16)
         total[...] += dot(inner, down_w[columns(i), :])
         if not last:
-            scores[1 - slot, 0:TILES, :] = later
+            scores[1 - slot] = later
 
     def feed_two(k, carry):
         feed(2 * k, 0, False)
         feed(2 * k + 1, 1, False)
         return carry
 
-    scores[0, 0:TILES, :] = dot(normed[...], up_w[:, columns(0)])
+    arrive(0)
+    scores[0] = dot(normed[...], up_w[:, columns(0)])
     lax.fori_loop(0, FF // FF_BLOCK // 2 - 1, feed_two, 0)
     feed(FF // FF_BLOCK - 2, 0, False)
     feed(FF // FF_BLOCK - 1, 1, True)
     tile_ref[...] = total[...].astype(BF16)
 
-    most = pl.ds(0, DEVICES - 1)
-    pltpu.make_async_copy(send1.at[most], send1.at[most], send1_sem).wait()
-    for c in range(3):
-        pltpu.make_async_copy(send2.at[c, most], send2.at[c, most], send2_sem.at[c]).wait()
-
-    most = far_recv.at[pl.ds(0, N_SEQ - 1)]
-    pltpu.make_async_copy(most, most, fsend_sem).wait()
-
-    @pl.when(sq // 16 == c0)
-    def _():
-        most = res_send.at[pl.ds(0, 15)]
-        pltpu.make_async_copy(most, most, rsend_sem).wait()
-
-    @pl.when(sq // 16 != c0)
-    def _():
-        pltpu.make_async_copy(res_send, res_send, rsend_sem).wait()
-
 
 def on_device(tile_feats, tile_dest, embed_weight, norm1_gain, qkv_weight, out_weight, norm2_gain, up_weight, down_weight):
     hbm = pl.BlockSpec(memory_space=pl.ANY)
     vmem = pl.BlockSpec(memory_space=pltpu.VMEM)
     dma = pltpu.SemaphoreType.DMA
-    tile_out, far_heads = pl.pallas_call(
+    state, results = pl.pallas_call(
         kernel,
         out_shape=(
             jax.ShapeDtypeStruct((TILES, D), BF16),
-            jax.ShapeDtypeStruct((HEADS, ROWS, HEAD), F32),
+            jax.ShapeDtypeStruct((HEADS, ROWS, 128), F32),
         ),
-        in_specs=[hbm, vmem, hbm, vmem, hbm, hbm, vmem, hbm, hbm],
+        in_specs=[hbm, vmem, hbm, vmem, hbm, hbm],
         out_specs=(vmem, vmem),
         scratch_shapes=[
             pltpu.VMEM((TILES, F), BF16),
             pltpu.VMEM((F, D), BF16),
             pltpu.VMEM((D, 3 * D), BF16),
             pltpu.VMEM((D, D), BF16),
-            pltpu.VMEM((D, FF), BF16),
-            pltpu.VMEM((FF, D), BF16),
             pltpu.VMEM((3 * D, D), BF16),
             pltpu.VMEM((TILES, D), BF16),
             pltpu.VMEM((TILES, D), BF16),
@@ -458,8 +477,7 @@
             pltpu.VMEM((3, DEVICES, 16, 128), BF16),
             pltpu.VMEM((3, DEVICES, 16, 128), BF16),
             pltpu.VMEM((TILES, D), F32),
-            pltpu.VMEM((TILES, D), F32),
-            dma((6,)),
+            dma((4,)),
             dma,
             dma((4,)),
             dma,
@@ -472,9 +490,26 @@
         ],
         compiler_params=pltpu.CompilerParams(collective_id=0, has_side_effects=True, vmem_limit_bytes=62 << 20),
     )(
-        tile_feats, tile_dest.reshape(1, TILES), embed_weight, norm1_gain, qkv_weight, out_weight,
-        norm2_gain, up_weight, down_weight,
+        tile_feats, tile_dest.reshape(1, TILES), embed_weight, norm1_gain, qkv_weight, out_weight
     )
+    tile_out, far_heads = pl.pallas_call(
+        feed_kernel,
+        out_shape=(
+            jax.ShapeDtypeStruct((TILES, D), BF16),
+            jax.ShapeDtypeStruct((HEADS, ROWS, HEAD), F32),
+        ),
+        in_specs=[vmem, vmem, vmem, hbm, hbm],
+        out_specs=(vmem, vmem),
+        scratch_shapes=[
+            pltpu.VMEM((D, FF), BF16),
+            pltpu.VMEM((FF, D), BF16),
+            pltpu.VMEM((TILES, D), BF16),
+            pltpu.VMEM((TILES, D), F32),
+            pltpu.VMEM((2, TILES, FF_BLOCK), F32),
+            dma((2, FF // FF_BLOCK)),
+        ],
+        compiler_params=pltpu.CompilerParams(vmem_limit_bytes=50 << 20),
+    )(state, results, norm2_gain, up_weight, down_weight)
     return tile_out, far_heads[None]
 
 

time: 85.6 us -> 86.4 us (level)
  Pallas kernels: 81.2 us -> 83.3 us
  local copies, waits for them, and re-layouts: 3.63 us -> 2.03 us
    pallas_call x0 -> x1, Pallas kernels: none -> 9.06 us  [on_device(): pl.pallas_call(feed_kernel, out_shape=(jax.ShapeDtypeStruct((TILES, D), B...]
    pallas_call x1, Pallas kernels: 81.2 us -> 74.2 us  [on_device(): pl.pallas_call(kernel, out_shape=(jax.ShapeDtypeStruct((TILES, D), BF16),...]
    unnamed x2 -> x6, local copies, waits for them, and re-layouts: 3.63 us -> 2.03 us
where the time goes in v3:
time: 86.4 us; the launch traced here: 86.2 us
  Pallas kernels  83.3 us (96%)
  local copies, waits for them, and re-layouts  2.03 us (2%)
    pallas_call x1, Pallas kernels, on_device(): pl.pallas_call(kernel, out_shape=(jax.ShapeDtypeStruct((TILES, D), BF16),...  74.2 us
    pallas_call x1, Pallas kernels, on_device(): pl.pallas_call(feed_kernel, out_shape=(jax.ShapeDtypeStruct((TILES, D), B...  9.06 us
    unnamed x6, local copies, waits for them, and re-layouts  2.03 us

profile of v3, /device:TPU:1, one launch (start us, length us, event | category | flops | bytes accessed | tf_op | source)
XLA Modules:
  0.0 86.2 jit_solution(4968959240625354686)
XLA Ops:
  0.6 0.0 copy-start.2
  0.6 74.2 %shard_map.104 = (bf16[512,768]{1,0:T(8,128)(2,1)}, f32[16,16,128]{2,1,0:T(8,128)}) custom-call(bf16[512,1536]{1,0:T(8,128)(2,1)} %feats_hbm.1, s32[1,512]{1,0:T(1,128)} %bitcast.2, bf16[1536,768]{1,0:T(8,128)(2,1)} %embed_hbm.1, f32[768]{0:T(1024)} %gain1_ref.1, bf16[768,2304]{1,0:T(8,128)(2,1)} %qkv_hbm.1, bf16[768,768]{1,0:T(8,128)(2,1)} %out_hbm.1), custom_call_target="tpu_custom_call" | custom-call | tf_op jit(solution)/shard_map/pallas_call | solution.py:445
  74.9 0.0 copy-done.2
  74.9 0.0 copy-start
  74.9 1.1 %copy-done = bf16[512,768]{1,0:T(8,128)(2,1)S(1)} copy-done((bf16[512,768]{1,0:T(8,128)(2,1)S(1)}, bf16[512,768]{1,0:T(8,128)(2,1)}, u32[]{:S(2)}) %copy-start) | copy-done | bytes 786456
  76.0 0.0 copy-start.1
  76.0 0.9 %copy-done.1 = f32[16,16,128]{2,1,0:T(8,128)S(1)} copy-done((f32[16,16,128]{2,1,0:T(8,128)S(1)}, f32[16,16,128]{2,1,0:T(8,128)}, u32[]{:S(2)}) %copy-start.1) | copy-done | bytes 131096
  76.9 9.1 %shard_map.105 = (bf16[512,768]{1,0:T(8,128)(2,1)}, f32[16,16,48]{2,1,0:T(8,128)}) custom-call(bf16[512,768]{1,0:T(8,128)(2,1)S(1)} %copy-done, f32[16,16,128]{2,1,0:T(8,128)S(1)} %copy-done.1, f32[768]{0:T(1024)S(1)} %copy-done.2, bf16[768,3072]{1,0:T(8,128)(2,1)} %up_hbm.1, bf16[3072,768]{1,0:T(8,128)(2,1)} %down_hbm.1), custom_call_target="tpu_custom_call" | custom-call | tf_op jit(solution)/shard_map/pallas_call | solution.py:495
Async XLA Ops:
  0.6 74.2 %copy-start.2 = (f32[768]{0:T(1024)S(1)}, f32[768]{0:T(1024)}, u32[]{:S(2)}) copy-start(f32[768]{0:T(1024)} %gain2_ref.1) | copy-start | bytes 9220
  74.9 1.1 %copy-start = (bf16[512,768]{1,0:T(8,128)(2,1)S(1)}, bf16[512,768]{1,0:T(8,128)(2,1)}, u32[]{:S(2)}) copy-start(bf16[512,768]{1,0:T(8,128)(2,1)} %get-tuple-element.6.state_ref) | copy-start | bytes 2359300
  76.0 0.9 %copy-start.1 = (f32[16,16,128]{2,1,0:T(8,128)S(1)}, f32[16,16,128]{2,1,0:T(8,128)}, u32[]{:S(2)}) copy-start(f32[16,16,128]{2,1,0:T(8,128)} %get-tuple-element.7.results_ref) | copy-start | bytes 393220
